TPU v7x, 32 devices: a whole 2x2x4 slice. The times are simulated.
32 devices in a mesh: groups: 2 (over y), tile: 4 (over z), chan: 2 (over x), sub: 2 (over core).
Axes of the slice: x: 2, y: 2, z: 4, core: 2. Of those that a mesh axis runs over, the one named last changes fastest.
Arguments:
- latent: bfloat16 [16, 8, 20, 512], P(('groups', 'sub'), None, 'tile', 'chan'), parts along dimension 0, may hold values from -34 to 34
- extents: int32 [4], replicated, may hold values from 1 to 4, as said below
- gain_one: float32 [512], P('chan'), may hold values from 0.1 to 1.9
- weight_one: bfloat16 [3, 3, 3, 512, 512], P(None, None, None, 'tile', 'chan'), may hold values from -0.0546875 to 0.0546875
- gain_two: float32 [512], P('chan'), may hold values from 0.1 to 1.9
- weight_two: bfloat16 [3, 3, 3, 512, 512], P(None, None, None, 'tile', 'chan'), may hold values from -0.0546875 to 0.0546875
Outputs:
- decoded: bfloat16 [16, 16, 40, 512], P(('groups', 'sub'), None, 'tile', 'chan'), parts along dimension 0
There are 2 independent parts, one for each index of `groups`. A program takes and returns all parts, laid end to end along the dimension named above; an argument that names none is the same for every part. Nothing has to cross between parts.
Inputs may be any that keep to these rules, and one draw needn't show every extreme that they name: `extents`: entry i is how many columns of tile i + 1 tile i decodes with its own; the last entry is not used. Among the used entries, the value 4 and the value 1 both occur.
All inputs are finite; a program needn't handle non-finite values.
Results may differ from a plain program's by a relative error of at most 0.0042.
Values may be sent and summed in bfloat16 or wider, within the bound.
A program may use at most 64 MiB of HBM per device.

v0:
```python
import jax
import jax.numpy as jnp
from jax import lax
from jax.sharding import PartitionSpec as P

CH = 512
GROUPS = 32
INTERSECTION = 4


eps = 1e-06


def shifted(array, axis, by):
    peers = lax.axis_size(axis)
    pairs = [(i, i + by) for i in range(peers) if 0 <= i + by < peers]
    return lax.ppermute(array, axis, pairs)


def convolve(inputs, kernel):
    result = lax.conv_general_dilated(
        inputs[None],
        kernel,
        (1, 1, 1),
        [(0, 0), (1, 1), (1, 1)],
        dimension_numbers=("NDHWC", "DHWIO", "NDHWC"),
        preferred_element_type=jnp.float32,
    )
    return result[0]


def group_norm(values, gain, count):
    group_size = CH // GROUPS
    grouped = values.reshape(values.shape[:-1] + (values.shape[-1] // group_size, group_size))
    totals, squares = lax.psum(
        (jnp.sum(grouped, axis=(0, 1, 2, 4)), jnp.sum(grouped * grouped, axis=(0, 1, 2, 4))), "sub"
    )
    size = count * group_size
    mean_val = totals / size
    variance = squares / size - mean_val * mean_val
    scaled = (grouped - mean_val[:, None]) * lax.rsqrt(variance + eps)[:, None]
    return scaled.reshape(values.shape) * gain


def causal_pad(values):
    earlier = shifted(values[-2:], "sub", 1)
    repeated = jnp.concatenate([values[:1], values[:1]], axis=0)
    leading = jnp.where(lax.axis_index("sub") == 0, repeated, earlier)
    return jnp.concatenate([leading, values], axis=0)


def blend_ramp(prior):
    positions = jnp.arange(2 * INTERSECTION).astype(jnp.float32) + 0.5
    limit = (2 * prior).astype(jnp.float32)[..., None]
    denom = (2 * jnp.maximum(prior, 1)).astype(jnp.float32)[..., None]
    return jnp.where(positions < limit, positions / denom, 1.0)


def channel_conv(padded_in, weight):
    full_in = lax.all_gather(padded_in, "chan", axis=3, tiled=True)
    out_count = weight.shape[4]
    share = weight.shape[3] // lax.axis_size("sub")
    portion = lax.dynamic_slice_in_dim(weight, lax.axis_index("sub") * share, share, 3)
    fetched = lax.all_gather(portion, "tile", axis=3, tiled=True)
    sectioned = fetched.reshape(3, 3, 3, lax.axis_size("tile"), 1, share, out_count)
    whole = lax.all_gather(sectioned, "sub", axis=4, tiled=True).reshape(3, 3, 3, -1, out_count)
    return convolve(full_in, whole)


def upscale(values):
    return jnp.repeat(jnp.repeat(values, 2, axis=1), 2, axis=2)


def shards(latent, extents, gain_one, weight_one, gain_two, weight_two):
    frame_count, row_count, col_count, chan_count = latent.shape
    tile_count = lax.axis_size("tile")
    place = lax.axis_index("tile")
    tile_ids = jnp.arange(tile_count, dtype=jnp.int32)
    reaches = jnp.where(tile_ids == tile_count - 1, 0, extents)
    reach = jnp.sum(jnp.where(tile_ids == place, reaches, 0))
    prior = jnp.sum(jnp.where(tile_ids == place - 1, reaches, 0))
    incoming = shifted(latent[:, :, :INTERSECTION, :], "tile", -1)
    window = jnp.concatenate([latent, incoming], axis=2)
    valid = (jnp.arange(col_count + INTERSECTION, dtype=jnp.int32) < col_count + reach).astype(
        jnp.float32
    )
    mask = valid[None, None, :, None]
    window = jnp.where(mask > 0, window, jnp.zeros_like(window))
    count = (col_count + reach).astype(jnp.float32) * (
        frame_count * lax.axis_size("sub") * row_count
    )
    source = window.astype(jnp.float32)
    hidden = (jax.nn.silu(group_norm(source, gain_one, count)) * mask).astype(jnp.bfloat16)
    first = (channel_conv(causal_pad(hidden), weight_one) * mask).astype(jnp.bfloat16)
    first = lax.optimization_barrier(first)
    hidden_two = (
        jax.nn.silu(group_norm(first.astype(jnp.float32), gain_two, count)) * mask
    ).astype(jnp.bfloat16)
    second = channel_conv(causal_pad(hidden_two), weight_two)
    result = ((source + second) * mask).astype(jnp.bfloat16)
    larger = upscale(result)
    own = larger[:, :, : 2 * col_count]
    arrived = shifted(larger[:, :, 2 * col_count :], "tile", 1)
    ramp = blend_ramp(prior)[None, None, :, None]
    head = own[:, :, : 2 * INTERSECTION].astype(jnp.float32) * ramp + arrived.astype(
        jnp.float32
    ) * (1.0 - ramp)
    return jnp.concatenate([head.astype(jnp.bfloat16), own[:, :, 2 * INTERSECTION :]], axis=2)


def solution(mesh):
    placed = (
        P(("groups", "sub"), None, "tile", "chan"),
        P(),
        P("chan"),
        P(None, None, None, "tile", "chan"),
        P("chan"),
        P(None, None, None, "tile", "chan"),
    )
    return jax.shard_map(
        shards,
        mesh=mesh,
        in_specs=placed,
        out_specs=P(("groups", "sub"), None, "tile", "chan"),
        check_vma=False,
    )
```

profile of v0, /device:TPU:0, one launch (start us, length us, event | category | flops | bytes accessed | tf_op | source)
XLA Modules:
  0.0 228.6 jit_solution(11239029631961013058)
XLA Ops:
  6.5 1.5 copy-done
  8.0 1.1 constant_dynamic-slice_fusion.1
  9.2 1.0 constant_dynamic-slice_fusion
  10.3 71.7 %all-gather.5.cloned.1.call-done = bf16[3,3,3,256,256]{4,3,2,1,0:T(8,128)(2,1)} async-done(((bf16[3,3,3,64,256]{4,3,2,1,0:T(8,128)(2,1)}), bf16[3,3,3,256,256]{4,3,2,1,0:T(8,128)(2,1)}) %all-gather.5.cloned.1.call-update) | async-done | bytes 3538960 | tf_op jit(solution)/shard_map/all_gather | solution.py:64
  82.1 1.3 collective-permute-start
  83.4 0.4 concatenate.27
  83.8 0.7 fusion.28
  85.2 3.0 %collective-permute-done = bf16[4,8,4,256]{3,1,2,0:T(8,128)(2,1)S(1)} collective-permute-done((bf16[4,8,4,256]{3,1,2,0:T(8,128)(2,1)S(1)}, bf16[4,8,4,256]{3,1,2,0:T(8,128)(2,1)S(1)}, u32[]{:S(2)}, u32[]{:S(2)}) %collective-permute-start) | collective-permute-done | bytes 65568 | tf_op jit(solution)/shard_map/ppermute | solution.py:17
  88.6 0.9 fusion
  89.5 2.5 %all-reduce.1 = (f32[16]{0:T(128)S(1)}, f32[16]{0:T(128)S(1)}) all-reduce(f32[16]{0:T(128)S(1)} %get-tuple-element.6, f32[16]{0:T(128)S(1)} %get-tuple-element.5), channel_id=1, replica_groups=mesh['groups'=2,'tile'=4,'chan'=2,'sub'=2] {'sub'}, use_global_device_ids=true, to_apply=%region_2.3 | all-reduce | flops 32 | bytes 256 | tf_op jit(solution)/shard_map/psum | solution.py:35
  92.5 2.1 collective-permute-start.1
  94.6 0.9 collective-permute-done.1
  95.6 8.4 %all_gather.18 = bf16[6,8,9,512]{3,1,2,0:T(8,128)(2,1)S(1)} all-gather(bf16[6,8,9,256]{3,1,2,0:T(8,128)(2,1)S(1)} %pad_maximum_fusion.1), channel_id=1, replica_groups=mesh['groups'=2,'tile'=4,'chan'=2,'sub'=2] {'chan'}, dimensions={3}, use_global_device_ids=true | all-gather | bytes 663552 | tf_op jit(solution)/shard_map/all_gather | solution.py:60
  103.9 48.2 %all-gather.9.cloned.1.call-done = bf16[3,3,3,256,256]{4,3,2,1,0:T(8,128)(2,1)} async-done(((bf16[3,3,3,64,256]{4,3,2,1,0:T(8,128)(2,1)}), bf16[3,3,3,256,256]{4,3,2,1,0:T(8,128)(2,1)}) %all-gather.9.cloned.1.call-update) | async-done | bytes 3538960 | tf_op jit(solution)/shard_map/all_gather | solution.py:64
  152.2 18.1 %all-gather.7.cloned.1.call-done = bf16[3,3,3,4,2,64,256]{6,5,4,3,2,1,0:T(8,128)(2,1)} async-done(((bf16[3,3,3,4,1,64,256]{6,5,4,3,2,1,0:T(8,128)(2,1)}), bf16[3,3,3,4,2,64,256]{6,5,4,3,2,1,0:T(8,128)(2,1)}) %all-gather.7.cloned.1.call-update) | async-done | bytes 7077904 | tf_op jit(solution)/shard_map/all_gather | solution.py:66
  170.3 13.1 %fusion.3 = f32[1,4,8,9,256]{4,0,3,2,1:T(1,128)S(1)} fusion(bf16[3,3,3,512,256]{4,3,2,1,0:T(8,128)(2,1)} %bitcast.36, bf16[1,6,8,9,512]{4,2,3,1,0:T(8,128)(2,1)S(1)} %bitcast.34), kind=kOutput, calls=%fused_computation.6 | convolution fusion | flops 1730150400 | bytes 7815168 | tf_op jit(solution)/shard_map/conv_general_dilated | solution.py:21
  183.9 2.5 %all-reduce = (f32[16]{0:T(128)S(1)}, f32[16]{0:T(128)S(1)}) all-reduce(f32[16]{0:T(128)S(1)} %reduce_sum.73, f32[16]{0:T(128)S(1)} %reduce_sum.76), channel_id=1, replica_groups=mesh['groups'=2,'tile'=4,'chan'=2,'sub'=2] {'sub'}, use_global_device_ids=true, to_apply=%region_7.8 | all-reduce | flops 32 | bytes 256 | tf_op jit(solution)/shard_map/psum | solution.py:35
  186.9 2.1 collective-permute-start.2
  189.0 1.0 collective-permute-done.2
  190.0 8.6 %all_gather.21 = bf16[6,8,9,512]{3,1,2,0:T(8,128)(2,1)S(1)} all-gather(bf16[6,8,9,256]{3,1,2,0:T(8,128)(2,1)S(1)} %pad_maximum_fusion.2), channel_id=1, replica_groups=mesh['groups'=2,'tile'=4,'chan'=2,'sub'=2] {'chan'}, dimensions={3}, use_global_device_ids=true | all-gather | bytes 663552 | tf_op jit(solution)/shard_map/all_gather | solution.py:60
  198.6 13.1 %fusion.1 = f32[1,4,8,9,256]{4,0,3,2,1:T(1,128)S(1)} fusion(bf16[3,3,3,512,256]{4,3,2,1,0:T(8,128)(2,1)} %bitcast.37, bf16[1,6,8,9,512]{4,2,3,1,0:T(8,128)(2,1)S(1)} %bitcast.35), kind=kOutput, calls=%fused_computation.4 | convolution fusion | flops 1730150400 | bytes 7815168 | tf_op jit(solution)/shard_map/conv_general_dilated | solution.py:21
  212.2 3.7 %collective-permute-start.3 = (bf16[4,16,8,256]{3,1,2,0:T(8,128)(2,1)S(1)}, bf16[4,16,8,256]{3,1,2,0:T(8,128)(2,1)S(1)}, u32[]{:S(2)}, u32[]{:S(2)}) collective-permute-start(bf16[4,16,8,256]{3,1,2,0:T(8,128)(2,1)S(1)} %slice.42), channel_id=1, source_target_pairs={{0,4},{4,8},{8,12},{1,5},{5,9},{9,13},{2,6},{6,10},{10,14},{3,7},{... | collective-permute-start | bytes 786440 | tf_op jit(solution)/shard_map/ppermute | solution.py:17
  217.3 3.9 %collective-permute-done.3 = bf16[4,16,8,256]{3,1,2,0:T(8,128)(2,1)S(1)} collective-permute-done((bf16[4,16,8,256]{3,1,2,0:T(8,128)(2,1)S(1)}, bf16[4,16,8,256]{3,1,2,0:T(8,128)(2,1)S(1)}, u32[]{:S(2)}, u32[]{:S(2)}) %collective-permute-start.3) | collective-permute-done | bytes 262176 | tf_op jit(solution)/shard_map/ppermute | solution.py:17
  221.3 0.8 pad_maximum_fusion
  (58 shorter events, 2.8 us)
Async XLA Ops:
  6.5 1.5 copy-start
  6.5 2.7 %copy-start.2 = (bf16[3,3,3,128,256]{4,3,2,1,0:T(8,128)(2,1)S(1)}, bf16[3,3,3,128,256]{4,3,2,1,0:T(8,128)(2,1)}, u32[]{:S(2)}) copy-start(bf16[3,3,3,128,256]{4,3,2,1,0:T(8,128)(2,1)} %param.11) | copy-start | bytes 5308420
  6.5 75.4 %all-gather.5.cloned.1.call-start = ((), (), s32[]{:S(2)}) async-start(), calls=%async_computation | async-start | bytes 4423680 | tf_op jit(solution)/shard_map/all_gather | solution.py:64
  9.2 143.0 %all-gather.9.cloned.1.call-start = ((), (), s32[]{:S(2)}) async-start(), calls=%async_computation.2 | async-start | bytes 4423680 | tf_op jit(solution)/shard_map/all_gather | solution.py:64
  10.2 71.8 %copy-start.1 = (bf16[4,8,5,256]{3,1,2,0:T(8,128)(2,1)S(1)}, bf16[4,8,5,256]{3,1,2,0:T(8,128)(2,1)}, u32[]{:S(2)}) copy-start(bf16[4,8,5,256]{3,1,2,0:T(8,128)(2,1)} %param.6) | copy-start | bytes 245764
  10.2 73.6 %copy-start.5 = (s32[4]{0:T(128)S(1)}, s32[4]{0:T(128)}, u32[]{:S(2)}) copy-start(s32[4]{0:T(128)} %param.7) | copy-start | bytes 52
  10.2 160.0 %all-gather.7.cloned.1.call-start = ((), (), s32[]{:S(2)}) async-start(), calls=%async_computation.1 | async-start | bytes 10616832 | tf_op jit(solution)/shard_map/all_gather | solution.py:66
  82.0 10.3 %copy-start.3 = (f32[256]{0:T(256)S(1)}, f32[256]{0:T(256)}, u32[]{:S(2)}) copy-start(f32[256]{0:T(256)} %param.8) | copy-start | bytes 3076
  82.0 116.7 %all-gather.11.cloned.1.call-start = ((), (), s32[]{:S(2)}) async-start(), calls=%async_computation.3 | async-start | bytes 10616832 | tf_op jit(solution)/shard_map/all_gather | solution.py:66
  82.1 6.2 %collective-permute-start = (bf16[4,8,4,256]{3,1,2,0:T(8,128)(2,1)S(1)}, bf16[4,8,4,256]{3,1,2,0:T(8,128)(2,1)S(1)}, u32[]{:S(2)}, u32[]{:S(2)}) collective-permute-start(bf16[4,8,4,256]{3,1,2,0:T(8,128)(2,1)S(1)} %slice.29), channel_id=1, source_target_pairs={{4,0},{8,4},{12,8},{5,1},{9,5},{13,9},{6,2},{10,6},{14,10},{7,3},{... | collective-permute-start | bytes 196616 | tf_op jit(solution)/shard_map/ppermute | solution.py:17
  92.5 3.0 %collective-permute-start.1 = (bf16[2,8,9,256]{3,1,2,0:T(8,128)(2,1)S(1)}, bf16[2,8,9,256]{3,1,2,0:T(8,128)(2,1)S(1)}, u32[]{:S(2)}, u32[]{:S(2)}) collective-permute-start(bf16[2,8,9,256]{3,1,2,0:T(8,128)(2,1)S(1)} %slice.38), channel_id=1, source_target_pairs={{0,1},{2,3},{4,5},{6,7},{8,9},{10,11},{12,13},{14,15},{16,17},{18,... | collective-permute-start | bytes 221192 | tf_op jit(solution)/shard_map/ppermute | solution.py:17
  170.3 16.4 %copy-start.4 = (f32[256]{0:T(256)S(1)}, f32[256]{0:T(256)}, u32[]{:S(2)}) copy-start(f32[256]{0:T(256)} %param.10) | copy-start | bytes 3076
  186.9 3.1 %collective-permute-start.2 = (bf16[2,8,9,256]{3,1,2,0:T(8,128)(2,1)S(1)}, bf16[2,8,9,256]{3,1,2,0:T(8,128)(2,1)S(1)}, u32[]{:S(2)}, u32[]{:S(2)}) collective-permute-start(bf16[2,8,9,256]{3,1,2,0:T(8,128)(2,1)S(1)} %slice.40), channel_id=1, source_target_pairs={{0,1},{2,3},{4,5},{6,7},{8,9},{10,11},{12,13},{14,15},{16,17},{18,... | collective-permute-start | bytes 221192 | tf_op jit(solution)/shard_map/ppermute | solution.py:17
  212.2 9.0 %collective-permute-start.3 = (bf16[4,16,8,256]{3,1,2,0:T(8,128)(2,1)S(1)}, bf16[4,16,8,256]{3,1,2,0:T(8,128)(2,1)S(1)}, u32[]{:S(2)}, u32[]{:S(2)}) collective-permute-start(bf16[4,16,8,256]{3,1,2,0:T(8,128)(2,1)S(1)} %slice.42), channel_id=1, source_target_pairs={{0,4},{4,8},{8,12},{1,5},{5,9},{9,13},{2,6},{6,10},{10,14},{3,7},{... | collective-permute-start | bytes 786440 | tf_op jit(solution)/shard_map/ppermute | solution.py:17
Sparse Core Ops, SparseCore 0:
  9.3 72.6 all-gather.4
  83.5 68.5 all-gather.8
  153.7 16.5 all-gather.6
  171.7 19.0 all-gather.10
where the time goes:
time: 229 us
  waiting for transfers between devices  147 us (64%)
  matrix products  26.2 us (11%)
  blocking collectives  21.9 us (10%)
  between operations  15.3 us (7%)
  starting transfers between devices  9.3 us (4%)
  local copies, waits for them, and re-layouts  5.55 us (2%)
  other arithmetic  3.47 us (2%)
    all_gather x2, waiting for transfers between devices, channel_conv(): fetched = lax.all_gather(portion, 'tile', axis=3, tiled=True)  120 us
    conv_general_dilated x2, matrix products, convolve(): lax.conv_general_dilated(inputs[None], kernel, (1, 1, 1), [(0, 0), (1, 1)...  26.2 us
    all_gather x2, waiting for transfers between devices, channel_conv(): lax.all_gather(sectioned, 'sub', axis=4, tiled=True)  18.1 us
    all_gather x2, blocking collectives, channel_conv(): full_in = lax.all_gather(padded_in, 'chan', axis=3, tiled=True)  17 us
    ppermute x4, starting transfers between devices, shifted(): return lax.ppermute(array, axis, pairs)  9.18 us
    ppermute x4, waiting for transfers between devices, shifted(): return lax.ppermute(array, axis, pairs)  8.8 us
    psum x2, blocking collectives, group_norm(): lax.psum((jnp.sum(grouped, axis=(0, 1, 2, 4)), jnp.sum(grouped * grouped,...  4.93 us
  transfers between devices with their start and end apart: 8, of which 7 were waited for; matrix products, arithmetic and copies ran while one was open for 8% of the time, Pallas kernels for 0%

commit v1 on v0

--- a/solution.py
+++ b/solution.py
@@ -67,6 +67,24 @@
     return convolve(full_in, whole)
 
 
+def stationary_conv(padded_in, weight):
+    tiles = lax.axis_size("tile")
+    share = weight.shape[3]
+    full_in = lax.all_gather(padded_in, "chan", axis=3, tiled=True)
+    split = full_in.reshape(full_in.shape[:3] + (tiles, share))
+    mine = lax.all_to_all(split, "tile", 3, 0, tiled=False)
+    partial = lax.conv_general_dilated(
+        mine,
+        weight,
+        (1, 1, 1),
+        [(0, 0), (1, 1), (1, 1)],
+        dimension_numbers=("NDHWC", "DHWIO", "NDHWC"),
+        preferred_element_type=jnp.float32,
+    ).astype(jnp.bfloat16)
+    back = lax.all_to_all(partial, "tile", 0, 0, tiled=True)
+    return jnp.sum(back.astype(jnp.float32), axis=0)
+
+
 def upscale(values):
     return jnp.repeat(jnp.repeat(values, 2, axis=1), 2, axis=2)
 
@@ -74,6 +92,7 @@
 def shards(latent, extents, gain_one, weight_one, gain_two, weight_two):
     frame_count, row_count, col_count, chan_count = latent.shape
     tile_count = lax.axis_size("tile")
+    conv = stationary_conv if weight_one.shape[3] % 128 == 0 else channel_conv
     place = lax.axis_index("tile")
     tile_ids = jnp.arange(tile_count, dtype=jnp.int32)
     reaches = jnp.where(tile_ids == tile_count - 1, 0, extents)
@@ -91,12 +110,12 @@
     )
     source = window.astype(jnp.float32)
     hidden = (jax.nn.silu(group_norm(source, gain_one, count)) * mask).astype(jnp.bfloat16)
-    first = (channel_conv(causal_pad(hidden), weight_one) * mask).astype(jnp.bfloat16)
+    first = (conv(causal_pad(hidden), weight_one) * mask).astype(jnp.bfloat16)
     first = lax.optimization_barrier(first)
     hidden_two = (
         jax.nn.silu(group_norm(first.astype(jnp.float32), gain_two, count)) * mask
     ).astype(jnp.bfloat16)
-    second = channel_conv(causal_pad(hidden_two), weight_two)
+    second = conv(causal_pad(hidden_two), weight_two)
     result = ((source + second) * mask).astype(jnp.bfloat16)
     larger = upscale(result)
     own = larger[:, :, : 2 * col_count]

time: 229 us -> 131 us (0.57)
  waiting for transfers between devices: 147 us -> 7.3 us
  blocking collectives: 21.9 us -> 96.8 us
  matrix products: 26.2 us -> 6.33 us
  between operations: 15.3 us -> 2.3 us
    all_gather x4 -> x0, waiting for transfers between devices: 138 us -> none  [the longest x2 120 us: channel_conv(): fetched = lax.all_gather(portion, 'tile', axis=3, tiled=True)]
    all_to_all x0 -> x4, blocking collectives: none -> 67.6 us  [the longest x2 35.3 us: stationary_conv(): back = lax.all_to_all(partial, 'tile', 0, 0, tiled=True)]
    conv_general_dilated x2, matrix products: 26.2 us -> 6.33 us  [stationary_conv(): lax.conv_general_dilated(mine, weight, (1, 1, 1), [(0, 0), (1, 1), (1, 1)...]
    all_gather x2, blocking collectives: 17 us -> 24.3 us  [stationary_conv(): full_in = lax.all_gather(padded_in, 'chan', axis=3, tiled=True)]
  transfers between devices with their start and end apart: 8 -> 4, of which waited for: 7 -> 4; matrix products, arithmetic and copies ran while one was open for 8% -> 2% of each run, Pallas kernels for 0% -> 0%
where the time goes in v1:
time: 131 us; the launch traced here: 130 us
  blocking collectives  96.8 us (74%)
  starting transfers between devices  7.76 us (6%)
  waiting for transfers between devices  7.3 us (6%)
  matrix products  6.33 us (5%)
  local copies, waits for them, and re-layouts  4.88 us (4%)
  other arithmetic  4.77 us (4%)
  between operations  2.3 us (2%)
    all_to_all x2, blocking collectives, stationary_conv(): back = lax.all_to_all(partial, 'tile', 0, 0, tiled=True)  35.3 us
    all_to_all x2, blocking collectives, stationary_conv(): mine = lax.all_to_all(split, 'tile', 3, 0, tiled=False)  32.3 us
    all_gather x2, blocking collectives, stationary_conv(): full_in = lax.all_gather(padded_in, 'chan', axis=3, tiled=True)  24.3 us
    ppermute x4, starting transfers between devices, shifted(): return lax.ppermute(array, axis, pairs)  7.76 us
    ppermute x4, waiting for transfers between devices, shifted(): return lax.ppermute(array, axis, pairs)  7.3 us
    conv_general_dilated x2, matrix products, stationary_conv(): lax.conv_general_dilated(mine, weight, (1, 1, 1), [(0, 0), (1, 1), (1, 1)...  6.33 us
    psum x2, blocking collectives, group_norm(): lax.psum((jnp.sum(grouped, axis=(0, 1, 2, 4)), jnp.sum(grouped * grouped,...  4.93 us
  transfers between devices with their start and end apart: 4, of which 4 were waited for; matrix products, arithmetic and copies ran while one was open for 2% of the time, Pallas kernels for 0%

profile of v1, /device:TPU:0, one launch (start us, length us, event | category | flops | bytes accessed | tf_op | source)
XLA Modules:
  0.0 130.2 jit_solution(4961865348018481005)
XLA Ops:
  0.0 1.1 copy.40
  1.1 1.3 collective-permute-start
  2.4 1.3 %concatenate.27 = bf16[4,8,5,16,16]{4,3,1,2,0:T(8,128)(2,1)S(1)} reshape(bf16[4,8,5,256]{3,1,2,0:T(8,128)(2,1)} %param.6) | data formatting | bytes 163840 | tf_op jit(solution)/shard_map/concatenate | solution.py:102
  3.8 1.4 %fusion.28 = (s32[]{:T(128)}, s32[]{:T(128)}) fusion(s32[]{:T(128)S(6)} %sub.53, s32[4]{0:T(128)} %param.7, s32[]{:T(128)S(6)} %axis_index.27), kind=kLoop, calls=%fused_computation.57 | loop fusion | flops 30 | bytes 32 | tf_op jit(solution)/shard_map/reduce_sum | solution.py:100
  5.8 2.4 %collective-permute-done = bf16[4,8,4,256]{3,2,1,0:T(4,128)(2,1)S(1)} collective-permute-done((bf16[4,8,4,256]{3,2,1,0:T(4,128)(2,1)S(1)}, bf16[4,8,4,256]{3,2,1,0:T(4,128)(2,1)S(1)}, u32[]{:S(2)}, u32[]{:S(2)}) %collective-permute-start) | collective-permute-done | bytes 65568 | tf_op jit(solution)/shard_map/ppermute | solution.py:17
  8.3 0.4 concatenate.28
  8.6 0.9 fusion
  9.6 2.5 %all-reduce.1 = (f32[16]{0:T(128)S(1)}, f32[16]{0:T(128)S(1)}) all-reduce(f32[16]{0:T(128)S(1)} %get-tuple-element.6, f32[16]{0:T(128)S(1)} %get-tuple-element.5), channel_id=1, replica_groups=mesh['groups'=2,'tile'=4,'chan'=2,'sub'=2] {'sub'}, use_global_device_ids=true, to_apply=%region_2.3 | all-reduce | flops 32 | bytes 256 | tf_op jit(solution)/shard_map/psum | solution.py:35
  12.7 2.1 %collective-permute-start.1 = (bf16[2,8,9,256]{3,2,1,0:T(8,128)(2,1)S(1)}, bf16[2,8,9,256]{3,2,1,0:T(8,128)(2,1)S(1)}, u32[]{:S(2)}, u32[]{:S(2)}) collective-permute-start(bf16[2,8,9,256]{3,2,1,0:T(8,128)(2,1)S(1)} %slice.39), channel_id=1, source_target_pairs={{0,1},{2,3},{4,5},{6,7},{8,9},{10,11},{12,13},{14,15},{16,17},{18,... | collective-permute-start | bytes 221192 | tf_op jit(solution)/shard_map/ppermute | solution.py:17
  14.8 0.9 collective-permute-done.1
  15.8 12.2 %all_gather.6 = bf16[6,8,9,512]{3,2,1,0:T(8,128)(2,1)S(1)} all-gather(bf16[6,8,9,256]{3,2,1,0:T(8,128)(2,1)S(1)} %pad_maximum_fusion), channel_id=1, replica_groups=mesh['groups'=2,'tile'=4,'chan'=2,'sub'=2] {'chan'}, dimensions={3}, use_global_device_ids=true | all-gather | bytes 663552 | tf_op jit(solution)/shard_map/all_gather | solution.py:73
  28.4 17.0 %all_to_all.40 = bf16[1,6,8,9,4,128]{5,2,3,1,0,4:T(8,128)(2,1)S(1)} all-to-all(bf16[1,6,8,9,4,128]{5,2,3,1,0,4:T(8,128)(2,1)S(1)} %copy.43), channel_id=1, replica_groups=mesh['groups'=2,'tile'=4,'chan'=2,'sub'=2] {'tile'}, dimensions={4} | all-to-all | bytes 884736 | tf_op jit(solution)/shard_map/all_to_all | solution.py:75
  45.5 3.2 %convolution_convert_fusion.1 = bf16[4,4,8,9,256]{4,0,3,2,1:T(4,128)(2,1)S(1)} fusion(bf16[3,3,3,128,256]{4,3,2,1,0:T(8,128)(2,1)S(1)} %copy-done, bf16[1,6,8,9,4,128]{5,2,3,1,0,4:T(8,128)(2,1)S(1)} %all_to_all.40), kind=kOutput, calls=%fused_computation.4 | convolution fusion | flops 1730445312 | bytes 2801664 | tf_op jit(solution)/shard_map/conv_general_dilated | solution.py:76
  48.7 17.7 %all_to_all.41 = bf16[4,4,8,9,256]{4,2,3,1,0:T(8,128)(2,1)S(1)} all-to-all(bf16[4,4,8,9,256]{4,2,3,1,0:T(8,128)(2,1)S(1)} %copy.45), channel_id=1, replica_groups=mesh['groups'=2,'tile'=4,'chan'=2,'sub'=2] {'tile'}, dimensions={0} | all-to-all | bytes 1179648 | tf_op jit(solution)/shard_map/all_to_all | solution.py:84
  67.1 2.5 %all-reduce = (f32[16]{0:T(128)S(1)}, f32[16]{0:T(128)S(1)}) all-reduce(f32[16]{0:T(128)S(1)} %reduce_sum.92, f32[16]{0:T(128)S(1)} %reduce_sum.95), channel_id=1, replica_groups=mesh['groups'=2,'tile'=4,'chan'=2,'sub'=2] {'sub'}, use_global_device_ids=true, to_apply=%region_8.9 | all-reduce | flops 32 | bytes 256 | tf_op jit(solution)/shard_map/psum | solution.py:35
  70.2 2.1 %collective-permute-start.2 = (bf16[2,8,9,256]{3,2,1,0:T(8,128)(2,1)S(1)}, bf16[2,8,9,256]{3,2,1,0:T(8,128)(2,1)S(1)}, u32[]{:S(2)}, u32[]{:S(2)}) collective-permute-start(bf16[2,8,9,256]{3,2,1,0:T(8,128)(2,1)S(1)} %slice.41), channel_id=1, source_target_pairs={{0,1},{2,3},{4,5},{6,7},{8,9},{10,11},{12,13},{14,15},{16,17},{18,... | collective-permute-start | bytes 221192 | tf_op jit(solution)/shard_map/ppermute | solution.py:17
  72.3 0.9 collective-permute-done.2
  73.3 12.1 %all_gather.7 = bf16[6,8,9,512]{3,2,1,0:T(8,128)(2,1)S(1)} all-gather(bf16[6,8,9,256]{3,2,1,0:T(8,128)(2,1)S(1)} %pad_maximum_fusion.1), channel_id=1, replica_groups=mesh['groups'=2,'tile'=4,'chan'=2,'sub'=2] {'chan'}, dimensions={3}, use_global_device_ids=true | all-gather | bytes 663552 | tf_op jit(solution)/shard_map/all_gather | solution.py:73
  85.7 15.2 %all_to_all.42 = bf16[1,6,8,9,4,128]{5,2,3,1,0,4:T(8,128)(2,1)S(1)} all-to-all(bf16[1,6,8,9,4,128]{5,2,3,1,0,4:T(8,128)(2,1)S(1)} %copy.48), channel_id=1, replica_groups=mesh['groups'=2,'tile'=4,'chan'=2,'sub'=2] {'tile'}, dimensions={4} | all-to-all | bytes 884736 | tf_op jit(solution)/shard_map/all_to_all | solution.py:75
  101.0 3.2 %convolution_convert_fusion = bf16[4,4,8,9,256]{4,0,3,2,1:T(4,128)(2,1)S(1)} fusion(bf16[3,3,3,128,256]{4,3,2,1,0:T(8,128)(2,1)S(1)} %copy-done.3, bf16[1,6,8,9,4,128]{5,2,3,1,0,4:T(8,128)(2,1)S(1)} %all_to_all.42), kind=kOutput, calls=%fused_computation.3 | convolution fusion | flops 1730445312 | bytes 2801664 | tf_op jit(solution)/shard_map/conv_general_dilated | solution.py:76
  104.2 17.6 %all_to_all.43 = bf16[4,4,8,9,256]{4,2,3,1,0:T(8,128)(2,1)S(1)} all-to-all(bf16[4,4,8,9,256]{4,2,3,1,0:T(8,128)(2,1)S(1)} %copy.50), channel_id=1, replica_groups=mesh['groups'=2,'tile'=4,'chan'=2,'sub'=2] {'tile'}, dimensions={0} | all-to-all | bytes 1179648 | tf_op jit(solution)/shard_map/all_to_all | solution.py:84
  122.6 2.3 %collective-permute-start.3 = (bf16[4,16,8,256]{3,1,2,0:T(8,128)(2,1)S(1)}, bf16[4,16,8,256]{3,1,2,0:T(8,128)(2,1)S(1)}, u32[]{:S(2)}, u32[]{:S(2)}) collective-permute-start(bf16[4,16,8,256]{3,1,2,0:T(8,128)(2,1)S(1)} %slice.43), channel_id=1, source_target_pairs={{0,4},{4,8},{8,12},{1,5},{5,9},{9,13},{2,6},{6,10},{10,14},{3,7},{... | collective-permute-start | bytes 786440 | tf_op jit(solution)/shard_map/ppermute | solution.py:17
  126.3 3.0 %collective-permute-done.3 = bf16[4,16,8,256]{3,1,2,0:T(8,128)(2,1)S(1)} collective-permute-done((bf16[4,16,8,256]{3,1,2,0:T(8,128)(2,1)S(1)}, bf16[4,16,8,256]{3,1,2,0:T(8,128)(2,1)S(1)}, u32[]{:S(2)}, u32[]{:S(2)}) %collective-permute-start.3) | collective-permute-done | bytes 262176 | tf_op jit(solution)/shard_map/ppermute | solution.py:17
  129.4 0.8 pad_maximum_fusion.2
  (53 shorter events, 3.8 us)
Async XLA Ops:
  0.0 45.5 %copy-start = (bf16[3,3,3,128,256]{4,3,2,1,0:T(8,128)(2,1)S(1)}, bf16[3,3,3,128,256]{4,3,2,1,0:T(8,128)(2,1)}, u32[]{:S(2)}) copy-start(bf16[3,3,3,128,256]{4,3,2,1,0:T(8,128)(2,1)} %param.9) | copy-start | bytes 5308420
  0.0 12.3 %copy-start.1 = (f32[256]{0:T(256)S(1)}, f32[256]{0:T(256)}, u32[]{:S(2)}) copy-start(f32[256]{0:T(256)} %param.8) | copy-start | bytes 3076
  1.1 7.2 %collective-permute-start = (bf16[4,8,4,256]{3,2,1,0:T(4,128)(2,1)S(1)}, bf16[4,8,4,256]{3,2,1,0:T(4,128)(2,1)S(1)}, u32[]{:S(2)}, u32[]{:S(2)}) collective-permute-start(bf16[4,8,4,256]{3,2,1,0:T(4,128)(2,1)S(1)} %slice.37), channel_id=1, source_target_pairs={{4,0},{8,4},{12,8},{5,1},{9,5},{13,9},{6,2},{10,6},{14,10},{7,3},{... | collective-permute-start | bytes 196616 | tf_op jit(solution)/shard_map/ppermute | solution.py:17
  12.7 3.0 %collective-permute-start.1 = (bf16[2,8,9,256]{3,2,1,0:T(8,128)(2,1)S(1)}, bf16[2,8,9,256]{3,2,1,0:T(8,128)(2,1)S(1)}, u32[]{:S(2)}, u32[]{:S(2)}) collective-permute-start(bf16[2,8,9,256]{3,2,1,0:T(8,128)(2,1)S(1)} %slice.39), channel_id=1, source_target_pairs={{0,1},{2,3},{4,5},{6,7},{8,9},{10,11},{12,13},{14,15},{16,17},{18,... | collective-permute-start | bytes 221192 | tf_op jit(solution)/shard_map/ppermute | solution.py:17
  48.7 21.2 %copy-start.2 = (f32[256]{0:T(256)S(1)}, f32[256]{0:T(256)}, u32[]{:S(2)}) copy-start(f32[256]{0:T(256)} %param.10) | copy-start | bytes 3076
  70.2 3.0 %collective-permute-start.2 = (bf16[2,8,9,256]{3,2,1,0:T(8,128)(2,1)S(1)}, bf16[2,8,9,256]{3,2,1,0:T(8,128)(2,1)S(1)}, u32[]{:S(2)}, u32[]{:S(2)}) collective-permute-start(bf16[2,8,9,256]{3,2,1,0:T(8,128)(2,1)S(1)} %slice.41), channel_id=1, source_target_pairs={{0,1},{2,3},{4,5},{6,7},{8,9},{10,11},{12,13},{14,15},{16,17},{18,... | collective-permute-start | bytes 221192 | tf_op jit(solution)/shard_map/ppermute | solution.py:17
  85.4 15.6 %copy-start.3 = (bf16[3,3,3,128,256]{4,3,2,1,0:T(8,128)(2,1)S(1)}, bf16[3,3,3,128,256]{4,3,2,1,0:T(8,128)(2,1)}, u32[]{:S(2)}) copy-start(bf16[3,3,3,128,256]{4,3,2,1,0:T(8,128)(2,1)} %param.11) | copy-start | bytes 5308420
  122.6 6.6 %collective-permute-start.3 = (bf16[4,16,8,256]{3,1,2,0:T(8,128)(2,1)S(1)}, bf16[4,16,8,256]{3,1,2,0:T(8,128)(2,1)S(1)}, u32[]{:S(2)}, u32[]{:S(2)}) collective-permute-start(bf16[4,16,8,256]{3,1,2,0:T(8,128)(2,1)S(1)} %slice.43), channel_id=1, source_target_pairs={{0,4},{4,8},{8,12},{1,5},{5,9},{9,13},{2,6},{6,10},{10,14},{3,7},{... | collective-permute-start | bytes 786440 | tf_op jit(solution)/shard_map/ppermute | solution.py:17

commit v2 on v0

--- a/solution.py
+++ b/solution.py
@@ -1,6 +1,10 @@
+import functools
+
 import jax
 import jax.numpy as jnp
 from jax import lax
+from jax.experimental import pallas as pl
+from jax.experimental.pallas import tpu as pltpu
 from jax.sharding import PartitionSpec as P
 
 CH = 512
@@ -108,6 +112,356 @@
     return jnp.concatenate([head.astype(jnp.bfloat16), own[:, :, 2 * INTERSECTION :]], axis=2)
 
 
+MESH = pl.DeviceIdType.MESH
+f32 = jnp.float32
+bf16 = jnp.bfloat16
+
+
+def block_kernel(dims, reach_ref, lat, gains, w_one, w_two, out, rx_one, rx_two, inc, gx, halo_one, halo_two,
+                 st_own_one, st_own_two, st_sib_one, st_sib_two, xs, hs, wv_one, wv_two, tx_one, tx_two, rp_one,
+                 rp_two, home, ys, tail, w_sem, dist_send, dist_recv, inc_sem, gain_send, gain_recv, halo_sem,
+                 st_sem, red_send, red_recv, tail_sem):
+    T, C, Q, B, F, R, KS, CL, span = dims
+    FR = F * R
+    pairs = T // 2
+    g, z, c, s = (lax.axis_index(a) for a in ("groups", "tile", "chan", "sub"))
+    sib = 1 - s
+    source = z // Q
+    size = CH // GROUPS
+
+    loads = [
+        pltpu.make_async_copy(w_one, wv_one, w_sem.at[0]),
+        pltpu.make_async_copy(w_two, wv_two, w_sem.at[1]),
+    ]
+    for load in loads:
+        load.start()
+
+    def remote(src, dst, send, recv, where):
+        return pltpu.make_async_remote_copy(
+            src_ref=src, dst_ref=dst, send_sem=send, recv_sem=recv, device_id=where, device_id_type=MESH
+        )
+
+    barrier = pltpu.get_barrier_semaphore()
+    for zz in range(T):
+        for cc in range(C):
+            @pl.when(jnp.logical_or(z != zz, c != cc))
+            def _():
+                pl.semaphore_signal(barrier, inc=1, device_id=(g, zz, cc, s), device_id_type=MESH)
+    pl.semaphore_signal(barrier, inc=1, device_id=(g, z, c, sib), device_id_type=MESH)
+    pl.semaphore_wait(barrier, T * C)
+
+    def send_parts(src, rx, k, finish):
+        for q in range(Q):
+            for cc in range(C):
+                zz = c * Q + q
+                there = jnp.logical_and(z == zz, c == cc)
+                move = remote(src.at[q], rx.at[z], dist_send.at[k, q * C + cc], dist_recv.at[k, z], (g, zz, cc, s))
+
+                @pl.when(jnp.logical_not(there))
+                def _():
+                    if finish:
+                        move.wait_send()
+                    else:
+                        move.start()
+
+                if not finish:
+                    @pl.when(there)
+                    def _():
+                        rx[z] = src[q]
+
+    def receive_parts(src, rx, k):
+        for t in range(T):
+            @pl.when(jnp.logical_or(z != t, source != c))
+            def _():
+                remote(src.at[0], rx.at[t], dist_send.at[k, 0], dist_recv.at[k, t], (g, z, c, sib)).wait_recv()
+
+    send_parts(lat, rx_one, 0, False)
+    edge = remote(lat.at[:, 0:INTERSECTION], inc, inc_sem.at[0], inc_sem.at[1], (g, jnp.maximum(z - 1, 0), c, s))
+
+    @pl.when(z > 0)
+    def _():
+        edge.start()
+
+    @pl.when(z == T - 1)
+    def _():
+        inc[...] = jnp.zeros_like(inc)
+
+    gx[c] = gains[...]
+    for cc in range(C):
+        @pl.when(c != cc)
+        def _():
+            remote(gains, gx.at[c], gain_send.at[cc], gain_recv.at[c], (g, z, cc, s)).start()
+
+    hs[...] = jnp.zeros_like(hs)
+
+    def reach_of(t):
+        return 0 if t == T - 1 else reach_ref[t]
+
+    my_reach = jnp.where(z == T - 1, 0, reach_ref[z])
+    prior = jnp.where(z == 0, 0, reach_ref[jnp.maximum(z - 1, 0)])
+
+    def valid(j, reach):
+        return jnp.where(j < B + reach, 1.0, 0.0).astype(f32)
+
+    def window_one(t, j):
+        if j >= B:
+            if t == T - 1:
+                return jnp.zeros((FR, KS), f32)
+            t, own, j, k = t + 1, t, j - B, j
+            return rx_one[t, j].astype(f32) * valid(k, reach_of(own))
+        return rx_one[t, j].astype(f32)
+
+    def window_two(t, j):
+        return rx_two[t, j].astype(f32)
+
+    lanes = lax.broadcasted_iota(jnp.int32, (2 * T * R, KS), 1)
+
+    def build(window, k, halo, st_own, st_sib):
+        for p in range(pairs):
+            total = jnp.zeros((F, 2 * R, KS), f32)
+            square = jnp.zeros((F, 2 * R, KS), f32)
+            for j in range(span):
+                low = window(2 * p, j).reshape(F, R, KS)
+                high = window(2 * p + 1, j).reshape(F, R, KS)
+                both = jnp.concatenate([low, high], axis=1)
+                total = total + both
+                square = square + both * both
+                xs[p, j] = both.astype(bf16)
+            st_own[0, pl.ds(2 * p * R, 2 * R)] = jnp.sum(total, axis=0)
+            st_own[1, pl.ds(2 * p * R, 2 * R)] = jnp.sum(square, axis=0)
+        stats = remote(st_own, st_sib, st_sem.at[k, 0], st_sem.at[k, 1], (g, z, c, sib))
+        stats.start()
+        edges = remote(xs.at[:, :, F - 2:F], halo, halo_sem.at[k, 0], halo_sem.at[k, 1], (g, z, c, sib))
+
+        @pl.when(s == 0)
+        def _():
+            edges.start()
+            first = xs[:, :, 0:1]
+            halo[:, :, 0:1] = first
+            halo[:, :, 1:2] = first
+
+        stats.wait()
+
+        @pl.when(s == 0)
+        def _():
+            edges.wait_send()
+
+        @pl.when(s == 1)
+        def _():
+            edges.wait_recv()
+
+        sums = (st_own[...] + st_sib[...]).reshape(2 * T, R, KS)
+        sums = jnp.broadcast_to(jnp.sum(sums, axis=1, keepdims=True), (2 * T, R, KS)).reshape(2 * T * R, KS)
+        step = 1
+        while step < size:
+            sums = sums + jnp.where(
+                (lanes & step) == 0, pltpu.roll(sums, KS - step, 1), pltpu.roll(sums, step, 1)
+            )
+            step *= 2
+        gain = gx[source, lax.rem(z, Q)][k:k + 1]
+        rows = lax.broadcasted_iota(jnp.int32, (1, R, KS), 1)
+        not_first = (rows > 0).astype(f32)
+        not_last = (rows < R - 1).astype(f32)
+        for p in range(pairs):
+            means, scales = [], []
+            for t in (2 * p, 2 * p + 1):
+                count = jnp.full((R, KS), (B + reach_of(t)), jnp.int32).astype(f32) * (2.0 * F * R * size)
+                mean = sums[t * R:(t + 1) * R] / count
+                var = sums[(T + t) * R:(T + t + 1) * R] / count - mean * mean
+                means.append(mean)
+                scales.append(lax.rsqrt(var + eps) * gain)
+            mean = jnp.concatenate(means, axis=0)
+            scale = jnp.concatenate(scales, axis=0)
+
+            def column(j, carry):
+                mask = jnp.concatenate(
+                    [jnp.full((R, KS), valid(j, reach_of(t)), f32) for t in (2 * p, 2 * p + 1)], axis=0
+                )
+                value = jnp.concatenate([halo[p, j], xs[p, j]], axis=0).astype(f32)
+                value = (value - mean) * scale
+                value = value / (1.0 + jnp.exp(-value)) * mask
+                hs[1, p, j + 1] = value.astype(bf16)
+                split = value.reshape((F + 2) * 2, R, KS)
+                down = pltpu.roll(split, 1, 1) * not_first
+                hs[0, p, j + 1] = down.reshape(F + 2, 2 * R, KS).astype(bf16)
+                up = pltpu.roll(split, R - 1, 1) * not_last
+                hs[2, p, j + 1] = up.reshape(F + 2, 2 * R, KS).astype(bf16)
+                return carry
+
+            lax.fori_loop(0, span, column, 0)
+
+    rows_m = span * F * 2 * R
+
+    def convolve_reduce(wv, k, tx, rp):
+        taps = [(a, b, d) for a in range(3) for b in range(3) for d in range(3)]
+
+        def pair(p, carry):
+            def patch(tap):
+                a, b, d = tap
+                return hs[b, p, d:d + span, a:a + F].reshape(rows_m, KS)
+
+            acc = None
+            for at in range(0, len(taps), 2):
+                chosen = taps[at:at + 2]
+                lhs = jnp.concatenate([patch(tap) for tap in chosen], axis=1)
+                term = jnp.dot(lhs, wv[at * KS:(at + len(chosen)) * KS], preferred_element_type=f32)
+                acc = term if acc is None else acc + term
+            acc = acc.reshape(span * F, 2 * R, CL)
+            for h in range(2):
+                t = 2 * p + h
+                tx[t] = acc[:, h * R:(h + 1) * R].reshape(span * FR, CL).astype(bf16)
+
+                @pl.when(t != z)
+                def _():
+                    remote(tx.at[t], rp.at[z], red_send.at[k, t], red_recv.at[k, z], (g, t, c, s)).start()
+
+            return carry
+
+        lax.fori_loop(0, pairs, pair, 0)
+        rp[z] = tx[z]
+        for t in range(T):
+            @pl.when(z != t)
+            def _():
+                move = remote(tx.at[t], rp.at[t], red_send.at[k, t], red_recv.at[k, t], (g, t, c, s))
+                move.wait_send()
+                move.wait_recv()
+
+    def summed(rp, j):
+        total = rp[0, j * FR:(j + 1) * FR].astype(f32)
+        for t in range(1, T):
+            total = total + rp[t, j * FR:(j + 1) * FR].astype(f32)
+        return total
+
+    receive_parts(lat, rx_one, 0)
+    for cc in range(C):
+        @pl.when(c != cc)
+        def _():
+            move = remote(gains, gx.at[cc], gain_send.at[cc], gain_recv.at[cc], (g, z, cc, s))
+            move.wait_send()
+            move.wait_recv()
+    build(window_one, 0, halo_one, st_own_one, st_sib_one)
+    loads[0].wait()
+    convolve_reduce(wv_one, 0, tx_one, rp_one)
+    for j in range(span):
+        row = (summed(rp_one, j) * valid(j, my_reach)).astype(bf16)
+        for q in range(Q):
+            home[q, j] = row[:, q * KS:(q + 1) * KS]
+    send_parts(home, rx_two, 1, False)
+    receive_parts(home, rx_two, 1)
+    build(window_two, 1, halo_two, st_own_two, st_sib_two)
+    loads[1].wait()
+    convolve_reduce(wv_two, 1, tx_two, rp_two)
+
+    @pl.when(z > 0)
+    def _():
+        edge.wait_send()
+
+    @pl.when(z < T - 1)
+    def _():
+        edge.wait_recv()
+
+    send_parts(lat, rx_one, 0, True)
+    send_parts(home, rx_two, 1, True)
+    for j in reversed(range(span)):
+        row = summed(rp_two, j)
+        for q in range(Q):
+            base = lat[q, j] if j < B else inc[q, j - B]
+            ys[q, j] = ((base.astype(f32) + row[:, q * KS:(q + 1) * KS]) * valid(j, my_reach)).astype(bf16)
+    spill = remote(
+        ys.at[:, B:span], tail, tail_sem.at[0], tail_sem.at[1], (g, jnp.minimum(z + 1, T - 1), c, s)
+    )
+
+    @pl.when(z < T - 1)
+    def _():
+        spill.start()
+
+    @pl.when(z == 0)
+    def _():
+        tail[...] = jnp.zeros_like(tail)
+
+    @pl.when(z > 0)
+    def _():
+        spill.wait_recv()
+
+    for j in range(2 * B):
+        if j < 2 * INTERSECTION:
+            limit = jnp.full((FR, KS), 2 * prior, jnp.int32).astype(f32)
+            spot = jnp.full((FR, KS), j + 0.5, f32)
+            ramp = jnp.where(spot < limit, spot / jnp.maximum(limit, 2.0), 1.0)
+            for q in range(Q):
+                mixed = ys[q, j // 2].astype(f32) * ramp + tail[q, j // 2].astype(f32) * (1.0 - ramp)
+                out[q, j] = mixed.astype(bf16)
+        else:
+            for q in range(Q):
+                out[q, j] = ys[q, j // 2]
+
+    @pl.when(z < T - 1)
+    def _():
+        spill.wait_send()
+
+
+def stationary(latent, extents, gain_one, weight_one, gain_two, weight_two):
+    F, R, B, CL = latent.shape
+    T, C = lax.axis_size("tile"), lax.axis_size("chan")
+    KS = weight_one.shape[3]
+    Q = CL // KS
+    span = B + INTERSECTION
+    FR = F * R
+    pairs = T // 2
+    lat = latent.reshape(FR, B, Q, KS).transpose(2, 1, 0, 3)
+    gains = jnp.stack([gain_one.reshape(Q, KS), gain_two.reshape(Q, KS)], axis=1)
+    gains = jnp.pad(gains, ((0, 0), (0, 6), (0, 0)))
+    taps = weight_one.shape[0] * weight_one.shape[1] * weight_one.shape[2]
+    w_one = weight_one.reshape(taps * KS, CL)
+    w_two = weight_two.reshape(taps * KS, CL)
+    vm = pltpu.VMEM
+    dma = pltpu.SemaphoreType.DMA
+    scratch = [
+        vm((T, B, FR, KS), bf16), vm((T, span, FR, KS), bf16), vm((Q, INTERSECTION, FR, KS), bf16),
+        vm((C, Q, 8, KS), f32),
+        vm((pairs, span, 2, 2 * R, KS), bf16), vm((pairs, span, 2, 2 * R, KS), bf16),
+        vm((2, T * R, KS), f32), vm((2, T * R, KS), f32), vm((2, T * R, KS), f32), vm((2, T * R, KS), f32),
+        vm((pairs, span, F, 2 * R, KS), bf16), vm((3, pairs, span + 2, F + 2, 2 * R, KS), bf16),
+        vm(w_one.shape, bf16), vm(w_two.shape, bf16),
+        vm((T, span * FR, CL), bf16), vm((T, span * FR, CL), bf16),
+        vm((T, span * FR, CL), bf16), vm((T, span * FR, CL), bf16),
+        vm((Q, span, FR, KS), bf16), vm((Q, span, FR, KS), bf16), vm((Q, INTERSECTION, FR, KS), bf16),
+        dma((2,)), dma((2, Q * C)), dma((2, T)), dma((2,)), dma((C,)), dma((C,)), dma((2, 2)), dma((2, 2)),
+        dma((2, T)), dma((2, T)), dma((2,)),
+    ]
+    whole = pl.BlockSpec(memory_space=pltpu.VMEM)
+    result = pl.pallas_call(
+        functools.partial(block_kernel, (T, C, Q, B, F, R, KS, CL, span)),
+        out_shape=jax.ShapeDtypeStruct((Q, 2 * B, FR, KS), bf16),
+        in_specs=[pl.BlockSpec(memory_space=pltpu.SMEM), whole, whole,
+                  pl.BlockSpec(memory_space=pl.ANY), pl.BlockSpec(memory_space=pl.ANY)],
+        out_specs=whole,
+        scratch_shapes=scratch,
+        compiler_params=pltpu.CompilerParams(
+            collective_id=0, has_side_effects=True, vmem_limit_bytes=48 * 1024 * 1024
+        ),
+    )(extents, lat, gains, w_one, w_two)
+    result = result.reshape(Q, 2 * B, F, R, KS).transpose(2, 3, 1, 0, 4).reshape(F, R, 2 * B, CL)
+    return jnp.repeat(result, 2, axis=1)
+
+
+def choose(latent, extents, gain_one, weight_one, gain_two, weight_two):
+    frames, rows, cols, chans = latent.shape
+    share = weight_one.shape[3]
+    fits = (
+        share % 128 == 0
+        and chans % share == 0
+        and lax.axis_size("tile") % 2 == 0
+        and lax.axis_size("sub") == 2
+        and rows == 8
+        and frames >= 2
+        and (frames * rows) % 16 == 0
+        and cols >= INTERSECTION
+    )
+    plan = stationary if fits else shards
+    return plan(latent, extents, gain_one, weight_one, gain_two, weight_two)
+
+
 def solution(mesh):
     placed = (
         P(("groups", "sub"), None, "tile", "chan"),
@@ -118,7 +472,7 @@
         P(None, None, None, "tile", "chan"),
     )
     return jax.shard_map(
-        shards,
+        choose,
         mesh=mesh,
         in_specs=placed,
         out_specs=P(("groups", "sub"), None, "tile", "chan"),

time: 229 us -> 72.4 us (0.32)
  the two profiles are of different devices: /device:TPU:0 before, /device:TPU:16 now
where the time goes in v2:
time: 72.4 us; the launch traced here: 72.2 us
  Pallas kernels  65.8 us (91%)
  local copies, waits for them, and re-layouts  5.62 us (8%)
    pallas_call x1, Pallas kernels, stationary(): pl.pallas_call(functools.partial(block_kernel, (T, C, Q, B, F, R, KS, CL,...  65.8 us
    unnamed x7, local copies, waits for them, and re-layouts  4.49 us

profile of v2, /device:TPU:16, one launch (start us, length us, event | category | flops | bytes accessed | tf_op | source)
XLA Modules:
  0.0 72.2 jit_solution(14937620549707521603)
XLA Ops:
  0.0 0.7 select_maximum_fusion.gains
  0.7 0.9 %copy.7 = bf16[4,8,5,256]{3,1,0,2:T(8,128)(2,1)S(1)} copy(bf16[4,8,5,256]{3,1,2,0:T(8,128)(2,1)} %param.6) | data formatting | bytes 163840 | tf_op args[0]
  1.6 0.0 copy-start
  1.7 1.5 %copy-done = bf16[3,3,3,128,256]{4,3,2,1,0:T(8,128)(2,1)S(1)} copy-done((bf16[3,3,3,128,256]{4,3,2,1,0:T(8,128)(2,1)S(1)}, bf16[3,3,3,128,256]{4,3,2,1,0:T(8,128)(2,1)}, u32[]{:S(2)}) %copy-start) | copy-done | bytes 1769496
  3.1 0.0 copy-start.1
  3.1 1.5 %copy-done.1 = bf16[3,3,3,128,256]{4,3,2,1,0:T(8,128)(2,1)S(1)} copy-done((bf16[3,3,3,128,256]{4,3,2,1,0:T(8,128)(2,1)S(1)}, bf16[3,3,3,128,256]{4,3,2,1,0:T(8,128)(2,1)}, u32[]{:S(2)}) %copy-start.1) | copy-done | bytes 1769496
  4.6 0.0 copy-start.2
  4.6 0.7 copy-done.2
  5.3 65.8 %shard_map.64 = bf16[2,10,32,128]{3,2,1,0:T(8,128)(2,1)S(1)} custom-call(s32[4]{0:T(128)S(1)} %copy-done.2, bf16[2,5,32,128]{3,2,1,0:T(8,128)(2,1)S(1)} %bitcast.22, f32[2,8,128]{2,1,0:T(8,128)S(1)} %select_maximum_fusion.gains, bf16[3456,256]{1,0:T(8,128)(2,1)S(1)} %bitcast.20, bf16[3456,256]{1,0:T(8,128)(2,1)S(1)} %bitcast.21), custom_call_target="tpu_custom_call" | custom-call | tf_op jit(solution)/shard_map/pallas_call | solution.py:433
  71.1 0.2 broadcast_in_dim.3
  71.3 0.9 %reshape.23 = bf16[4,16,10,256]{3,1,2,0:T(8,128)(2,1)} reshape(bf16[4,8,2,10,256]{4,2,1,3,0:T(2,128)(2,1)S(1)} %broadcast_in_dim.3) | data formatting | bytes 655360 | tf_op jit(solution)/shard_map/reshape | solution.py:445
  (3 shorter events, 0.1 us)
Async XLA Ops:
  1.6 1.5 %copy-start = (bf16[3,3,3,128,256]{4,3,2,1,0:T(8,128)(2,1)S(1)}, bf16[3,3,3,128,256]{4,3,2,1,0:T(8,128)(2,1)}, u32[]{:S(2)}) copy-start(bf16[3,3,3,128,256]{4,3,2,1,0:T(8,128)(2,1)} %param.9) | copy-start | bytes 5308420
  3.1 1.5 %copy-start.1 = (bf16[3,3,3,128,256]{4,3,2,1,0:T(8,128)(2,1)S(1)}, bf16[3,3,3,128,256]{4,3,2,1,0:T(8,128)(2,1)}, u32[]{:S(2)}) copy-start(bf16[3,3,3,128,256]{4,3,2,1,0:T(8,128)(2,1)} %param.11) | copy-start | bytes 5308420
  4.6 0.7 copy-start.2

commit v3 on v2

--- a/solution.py
+++ b/solution.py
@@ -118,8 +118,8 @@
 
 
 def block_kernel(dims, reach_ref, lat, gains, w_one, w_two, out, rx_one, rx_two, inc, gx, halo_one, halo_two,
-                 st_own_one, st_own_two, st_sib_one, st_sib_two, xs, hs, wv_one, wv_two, tx_one, tx_two, rp_one,
-                 rp_two, home, ys, tail, w_sem, dist_send, dist_recv, inc_sem, gain_send, gain_recv, halo_sem,
+                 st_own_one, st_own_two, st_sib_one, st_sib_two, xs, hs, wv_one, wv_two, tx_one, tx_two, near_one,
+                 near_two, rp_one, rp_two, home, ys, tail, w_sem, dist_send, dist_recv, fwd_send, inc_sem, gain_send, gain_recv, halo_sem,
                  st_sem, red_send, red_recv, tail_sem):
     T, C, Q, B, F, R, KS, CL, span = dims
     FR = F * R
@@ -127,6 +127,8 @@
     g, z, c, s = (lax.axis_index(a) for a in ("groups", "tile", "chan", "sub"))
     sib = 1 - s
     source = z // Q
+    block, odd = z // 2, lax.rem(z, 2)
+    partner = z + 1 - 2 * odd
     size = CH // GROUPS
 
     loads = [
@@ -152,27 +154,52 @@
 
     def send_parts(src, rx, k, finish):
         for q in range(Q):
-            for cc in range(C):
-                zz = c * Q + q
-                there = jnp.logical_and(z == zz, c == cc)
-                move = remote(src.at[q], rx.at[z], dist_send.at[k, q * C + cc], dist_recv.at[k, z], (g, zz, cc, s))
-
-                @pl.when(jnp.logical_not(there))
+            zz = c * Q + q
+            move = remote(src.at[q], rx.at[z], dist_send.at[k, q], dist_recv.at[k, z], (g, zz, c, s))
+
+            @pl.when(z != zz)
+            def _():
+                if finish:
+                    move.wait_send()
+                else:
+                    move.start()
+
+            if not finish:
+                @pl.when(z == zz)
                 def _():
-                    if finish:
-                        move.wait_send()
-                    else:
-                        move.start()
-
-                if not finish:
-                    @pl.when(there)
-                    def _():
-                        rx[z] = src[q]
+                    rx[z] = src[q]
+        if finish:
+            @pl.when(source == c)
+            def _():
+                for t in range(T):
+                    for off in range(1, C):
+                        onward(rx, k, t, off).wait_send()
+
+    def onward(rx, k, t, off):
+        there = (g, z, lax.rem(c + off, C), s)
+        return remote(rx.at[t], rx.at[t], fwd_send.at[k, off, t], dist_recv.at[k, t], there)
 
     def receive_parts(src, rx, k):
-        for t in range(T):
-            @pl.when(jnp.logical_or(z != t, source != c))
+        steps = [0]
+        for far in range(1, T):
+            steps += [far, -far]
+        for far in steps:
+            t = z + far
+
+            @pl.when(jnp.logical_and(t >= 0, t < T))
             def _():
+                arrival = remote(src.at[0], rx.at[t], dist_send.at[k, 0], dist_recv.at[k, t], (g, z, c, sib))
+
+                @pl.when(source == c)
+                def _():
+                    if far != 0:
+                        arrival.wait_recv()
+                    for off in range(1, C):
+                        onward(rx, k, t, off).start()
+
+        @pl.when(source != c)
+        def _():
+            for t in range(T):
                 remote(src.at[0], rx.at[t], dist_send.at[k, 0], dist_recv.at[k, t], (g, z, c, sib)).wait_recv()
 
     send_parts(lat, rx_one, 0, False)
@@ -292,10 +319,12 @@
 
     rows_m = span * F * 2 * R
 
-    def convolve_reduce(wv, k, tx, rp):
+    def convolve_reduce(wv, k, tx, near, rp):
         taps = [(a, b, d) for a in range(3) for b in range(3) for d in range(3)]
 
-        def pair(p, carry):
+        def pair(i, carry):
+            p = lax.rem(block + 1 + i, pairs)
+
             def patch(tap):
                 a, b, d = tap
                 return hs[b, p, d:d + span, a:a + F].reshape(rows_m, KS)
@@ -308,28 +337,43 @@
                 acc = term if acc is None else acc + term
             acc = acc.reshape(span * F, 2 * R, CL)
             for h in range(2):
-                t = 2 * p + h
-                tx[t] = acc[:, h * R:(h + 1) * R].reshape(span * FR, CL).astype(bf16)
-
-                @pl.when(t != z)
-                def _():
-                    remote(tx.at[t], rp.at[z], red_send.at[k, t], red_recv.at[k, z], (g, t, c, s)).start()
-
+                tx[2 * p + h] = acc[:, h * R:(h + 1) * R].reshape(span * FR, CL).astype(bf16)
+            handed(p).start()
             return carry
 
+        def handed(p):
+            return remote(
+                tx.at[2 * p + 1 - odd], near.at[p], red_send.at[k, p], red_recv.at[k, p], (g, partner, c, s)
+            )
+
+        def combined(p):
+            t = 2 * p + odd
+            return remote(
+                tx.at[t], rp.at[block], red_send.at[k, pairs + p], red_recv.at[k, pairs + block], (g, t, c, s)
+            )
+
         lax.fori_loop(0, pairs, pair, 0)
-        rp[z] = tx[z]
-        for t in range(T):
-            @pl.when(z != t)
-            def _():
-                move = remote(tx.at[t], rp.at[t], red_send.at[k, t], red_recv.at[k, t], (g, t, c, s))
-                move.wait_send()
-                move.wait_recv()
-
-    def summed(rp, j):
-        total = rp[0, j * FR:(j + 1) * FR].astype(f32)
-        for t in range(1, T):
-            total = total + rp[t, j * FR:(j + 1) * FR].astype(f32)
+        rp[block] = tx[z]
+        for i in range(pairs):
+            p = lax.rem(block + 1 + i, pairs)
+            handed(p).wait_recv()
+            if i < pairs - 1:
+                t = 2 * p + odd
+                tx[t] = (tx[t].astype(f32) + near[p].astype(f32)).astype(bf16)
+                combined(p).start()
+        for i in range(pairs):
+            p = lax.rem(block + 1 + i, pairs)
+            handed(p).wait_send()
+            if i < pairs - 1:
+                combined(p).wait_send()
+                remote(
+                    tx.at[z], rp.at[p], red_send.at[k, pairs + p], red_recv.at[k, pairs + p], (g, partner, c, s)
+                ).wait_recv()
+
+    def summed(near, rp, j):
+        total = near[block, j * FR:(j + 1) * FR].astype(f32)
+        for m in range(pairs):
+            total = total + rp[m, j * FR:(j + 1) * FR].astype(f32)
         return total
 
     receive_parts(lat, rx_one, 0)
@@ -341,16 +385,16 @@
             move.wait_recv()
     build(window_one, 0, halo_one, st_own_one, st_sib_one)
     loads[0].wait()
-    convolve_reduce(wv_one, 0, tx_one, rp_one)
+    convolve_reduce(wv_one, 0, tx_one, near_one, rp_one)
     for j in range(span):
-        row = (summed(rp_one, j) * valid(j, my_reach)).astype(bf16)
+        row = (summed(near_one, rp_one, j) * valid(j, my_reach)).astype(bf16)
         for q in range(Q):
             home[q, j] = row[:, q * KS:(q + 1) * KS]
     send_parts(home, rx_two, 1, False)
     receive_parts(home, rx_two, 1)
     build(window_two, 1, halo_two, st_own_two, st_sib_two)
     loads[1].wait()
-    convolve_reduce(wv_two, 1, tx_two, rp_two)
+    convolve_reduce(wv_two, 1, tx_two, near_two, rp_two)
 
     @pl.when(z > 0)
     def _():
@@ -363,7 +407,7 @@
     send_parts(lat, rx_one, 0, True)
     send_parts(home, rx_two, 1, True)
     for j in reversed(range(span)):
-        row = summed(rp_two, j)
+        row = summed(near_two, rp_two, j)
         for q in range(Q):
             base = lat[q, j] if j < B else inc[q, j - B]
             ys[q, j] = ((base.astype(f32) + row[:, q * KS:(q + 1) * KS]) * valid(j, my_reach)).astype(bf16)
@@ -424,9 +468,10 @@
         vm((pairs, span, F, 2 * R, KS), bf16), vm((3, pairs, span + 2, F + 2, 2 * R, KS), bf16),
         vm(w_one.shape, bf16), vm(w_two.shape, bf16),
         vm((T, span * FR, CL), bf16), vm((T, span * FR, CL), bf16),
-        vm((T, span * FR, CL), bf16), vm((T, span * FR, CL), bf16),
+        vm((pairs, span * FR, CL), bf16), vm((pairs, span * FR, CL), bf16),
+        vm((pairs, span * FR, CL), bf16), vm((pairs, span * FR, CL), bf16),
         vm((Q, span, FR, KS), bf16), vm((Q, span, FR, KS), bf16), vm((Q, INTERSECTION, FR, KS), bf16),
-        dma((2,)), dma((2, Q * C)), dma((2, T)), dma((2,)), dma((C,)), dma((C,)), dma((2, 2)), dma((2, 2)),
+        dma((2,)), dma((2, Q)), dma((2, T)), dma((2, C, T)), dma((2,)), dma((C,)), dma((C,)), dma((2, 2)), dma((2, 2)),
         dma((2, T)), dma((2, T)), dma((2,)),
     ]
     whole = pl.BlockSpec(memory_space=pltpu.VMEM)
@@ -438,7 +483,7 @@
         out_specs=whole,
         scratch_shapes=scratch,
         compiler_params=pltpu.CompilerParams(
-            collective_id=0, has_side_effects=True, vmem_limit_bytes=48 * 1024 * 1024
+            collective_id=0, has_side_effects=True, vmem_limit_bytes=60 * 1024 * 1024
         ),
     )(extents, lat, gains, w_one, w_two)
     result = result.reshape(Q, 2 * B, F, R, KS).transpose(2, 3, 1, 0, 4).reshape(F, R, 2 * B, CL)

time: 72.4 us -> 68 us (0.939)
  the two profiles are of different devices: /device:TPU:16 before, /device:TPU:0 now
where the time goes in v3:
time: 68 us; the launch traced here: 67.8 us
  Pallas kernels  62.9 us (92%)
  local copies, waits for them, and re-layouts  3.57 us (5%)
  other arithmetic  1.3 us (2%)
    pallas_call x1, Pallas kernels, stationary(): pl.pallas_call(functools.partial(block_kernel, (T, C, Q, B, F, R, KS, CL,...  62.9 us

profile of v3, /device:TPU:0, one launch (start us, length us, event | category | flops | bytes accessed | tf_op | source)
XLA Modules:
  0.0 67.8 jit_solution(16683980097833261154)
XLA Ops:
  0.0 1.3 %select_maximum_fusion.gains = f32[2,8,128]{2,1,0:T(8,128)} fusion(f32[2,1,128]{2,1,0:T(1,128)} %bitcast.23, f32[2,1,128]{2,1,0:T(1,128)} %bitcast.24), kind=kLoop, calls=%fused_computation.2 | loop fusion | flops 8192 | bytes 10240 | tf_op jit(solution)/shard_map/stack | solution.py:456
  1.3 0.9 %copy.7 = bf16[4,8,5,256]{3,1,0,2:T(8,128)(2,1)S(1)} copy(bf16[4,8,5,256]{3,1,2,0:T(8,128)(2,1)} %param.6) | data formatting | bytes 163840 | tf_op args[0]
  2.2 0.7 copy.12
  2.9 62.9 %shard_map.64 = bf16[2,10,32,128]{3,2,1,0:T(8,128)(2,1)} custom-call(s32[4]{0:T(128)} %reach_ref.1, bf16[2,5,32,128]{3,2,1,0:T(8,128)(2,1)} %bitcast.22, f32[2,8,128]{2,1,0:T(8,128)} %select_maximum_fusion.gains, bf16[3456,256]{1,0:T(8,128)(2,1)} %bitcast.20, bf16[3456,256]{1,0:T(8,128)(2,1)} %bitcast.21), custom_call_target="tpu_custom_call" | custom-call | tf_op jit(solution)/shard_map/pallas_call | solution.py:478
  65.8 0.9 %copy_bitcast_fusion = bf16[4,8,10,256]{3,1,2,0:T(8,128)(2,1)S(1)} fusion(bf16[2,10,32,128]{3,2,1,0:T(8,128)(2,1)} %shard_map.64), kind=kLoop, calls=%fused_computation | loop fusion | bytes 327680 | tf_op jit(solution)/shard_map/reshape | solution.py:489
  66.7 0.2 broadcast_in_dim.3
  67.0 0.9 %reshape.23 = bf16[4,16,10,256]{3,1,2,0:T(8,128)(2,1)} reshape(bf16[4,8,2,10,256]{4,2,1,3,0:T(2,128)(2,1)S(1)} %broadcast_in_dim.3) | data formatting | bytes 655360 | tf_op jit(solution)/shard_map/reshape | solution.py:490
  (1 shorter events, 0.0 us)

commit v4 on v3

--- a/solution.py
+++ b/solution.py
@@ -152,13 +152,20 @@
     pl.semaphore_signal(barrier, inc=1, device_id=(g, z, c, sib), device_id_type=MESH)
     pl.semaphore_wait(barrier, T * C)
 
-    def send_parts(src, rx, k, finish):
+    def pieces(columns):
+        return 3 if columns % 3 == 0 else 1
+
+    def send_piece(src, rx, k, ch, finish):
+        width = rx.shape[1] // pieces(rx.shape[1])
+        cut = pl.ds(ch * width, width)
         for q in range(Q):
             zz = c * Q + q
-            move = remote(src.at[q], rx.at[z], dist_send.at[k, q], dist_recv.at[k, z], (g, zz, c, s))
 
             @pl.when(z != zz)
             def _():
+                move = remote(
+                    src.at[q, cut], rx.at[z, cut], dist_send.at[k, q, ch], dist_recv.at[k, z, ch], (g, zz, c, s)
+                )
                 if finish:
                     move.wait_send()
                 else:
@@ -167,42 +174,47 @@
             if not finish:
                 @pl.when(z == zz)
                 def _():
-                    rx[z] = src[q]
-        if finish:
+                    rx[z, cut] = src[q, cut]
+
+    def onward(rx, k, t, off, ch):
+        width = rx.shape[1] // pieces(rx.shape[1])
+        part = rx.at[t, pl.ds(ch * width, width)]
+        there = (g, z, lax.rem(c + off, C), s)
+        return remote(part, part, fwd_send.at[k, off, t, ch], dist_recv.at[k, t, ch], there)
+
+    def finish_parts(src, rx, k):
+        for ch in range(pieces(rx.shape[1])):
+            send_piece(src, rx, k, ch, True)
+
             @pl.when(source == c)
             def _():
                 for t in range(T):
                     for off in range(1, C):
-                        onward(rx, k, t, off).wait_send()
-
-    def onward(rx, k, t, off):
-        there = (g, z, lax.rem(c + off, C), s)
-        return remote(rx.at[t], rx.at[t], fwd_send.at[k, off, t], dist_recv.at[k, t], there)
+                        onward(rx, k, t, off, ch).wait_send()
 
     def receive_parts(src, rx, k):
         steps = [0]
         for far in range(1, T):
             steps += [far, -far]
-        for far in steps:
-            t = z + far
-
-            @pl.when(jnp.logical_and(t >= 0, t < T))
-            def _():
-                arrival = remote(src.at[0], rx.at[t], dist_send.at[k, 0], dist_recv.at[k, t], (g, z, c, sib))
-
-                @pl.when(source == c)
+        for ch in range(pieces(rx.shape[1])):
+            for far in steps:
+                t = z + far
+
+                @pl.when(jnp.logical_and(source == c, jnp.logical_and(t >= 0, t < T)))
                 def _():
                     if far != 0:
-                        arrival.wait_recv()
+                        onward(rx, k, t, 0, ch).wait_recv()
                     for off in range(1, C):
-                        onward(rx, k, t, off).start()
+                        onward(rx, k, t, off, ch).start()
 
         @pl.when(source != c)
         def _():
-            for t in range(T):
-                remote(src.at[0], rx.at[t], dist_send.at[k, 0], dist_recv.at[k, t], (g, z, c, sib)).wait_recv()
-
-    send_parts(lat, rx_one, 0, False)
+            for ch in range(pieces(rx.shape[1])):
+                for t in range(T):
+                    onward(rx, k, t, 0, ch).wait_recv()
+
+    for ch in range(pieces(B)):
+        send_piece(lat, rx_one, 0, ch, False)
     edge = remote(lat.at[:, 0:INTERSECTION], inc, inc_sem.at[0], inc_sem.at[1], (g, jnp.maximum(z - 1, 0), c, s))
 
     @pl.when(z > 0)
@@ -322,6 +334,23 @@
     def convolve_reduce(wv, k, tx, near, rp):
         taps = [(a, b, d) for a in range(3) for b in range(3) for d in range(3)]
 
+        def chunk(ch):
+            rows = span // pieces(span) * FR
+            return pl.ds(ch * rows, rows)
+
+        def handed(p, ch):
+            return remote(
+                tx.at[2 * p + 1 - odd, chunk(ch)], near.at[p, chunk(ch)], red_send.at[k, p, ch],
+                red_recv.at[k, p, ch], (g, partner, c, s)
+            )
+
+        def combined(p, ch):
+            t = 2 * p + odd
+            return remote(
+                tx.at[t, chunk(ch)], rp.at[block, chunk(ch)], red_send.at[k, pairs + p, ch],
+                red_recv.at[k, pairs + block, ch], (g, t, c, s)
+            )
+
         def pair(i, carry):
             p = lax.rem(block + 1 + i, pairs)
 
@@ -338,37 +367,43 @@
             acc = acc.reshape(span * F, 2 * R, CL)
             for h in range(2):
                 tx[2 * p + h] = acc[:, h * R:(h + 1) * R].reshape(span * FR, CL).astype(bf16)
-            handed(p).start()
+
+            @pl.when(i < pairs - 1)
+            def _():
+                for ch in range(pieces(span)):
+                    handed(p, ch).start()
+
             return carry
-
-        def handed(p):
-            return remote(
-                tx.at[2 * p + 1 - odd], near.at[p], red_send.at[k, p], red_recv.at[k, p], (g, partner, c, s)
-            )
-
-        def combined(p):
-            t = 2 * p + odd
-            return remote(
-                tx.at[t], rp.at[block], red_send.at[k, pairs + p], red_recv.at[k, pairs + block], (g, t, c, s)
-            )
 
         lax.fori_loop(0, pairs, pair, 0)
         rp[block] = tx[z]
-        for i in range(pairs):
-            p = lax.rem(block + 1 + i, pairs)
-            handed(p).wait_recv()
-            if i < pairs - 1:
+        for ch in range(pieces(span)):
+            for i in range(pairs - 1):
+                p = lax.rem(block + 1 + i, pairs)
+                handed(p, ch).wait_recv()
                 t = 2 * p + odd
-                tx[t] = (tx[t].astype(f32) + near[p].astype(f32)).astype(bf16)
-                combined(p).start()
-        for i in range(pairs):
-            p = lax.rem(block + 1 + i, pairs)
-            handed(p).wait_send()
-            if i < pairs - 1:
-                combined(p).wait_send()
+                tx[t, chunk(ch)] = (tx[t, chunk(ch)].astype(f32) + near[p, chunk(ch)].astype(f32)).astype(bf16)
+                combined(p, ch).start()
+            handed(block, ch).start()
+
+        def arrive(ch):
+            handed(block, ch).wait_recv()
+            for i in range(pairs - 1):
+                p = lax.rem(block + 1 + i, pairs)
                 remote(
-                    tx.at[z], rp.at[p], red_send.at[k, pairs + p], red_recv.at[k, pairs + p], (g, partner, c, s)
+                    tx.at[z, chunk(ch)], rp.at[p, chunk(ch)], red_send.at[k, pairs + p, ch],
+                    red_recv.at[k, pairs + p, ch], (g, partner, c, s)
                 ).wait_recv()
+
+        def close():
+            for ch in range(pieces(span)):
+                for i in range(pairs):
+                    p = lax.rem(block + 1 + i, pairs)
+                    handed(p, ch).wait_send()
+                    if i < pairs - 1:
+                        combined(p, ch).wait_send()
+
+        return arrive, close
 
     def summed(near, rp, j):
         total = near[block, j * FR:(j + 1) * FR].astype(f32)
@@ -385,16 +420,19 @@
             move.wait_recv()
     build(window_one, 0, halo_one, st_own_one, st_sib_one)
     loads[0].wait()
-    convolve_reduce(wv_one, 0, tx_one, near_one, rp_one)
-    for j in range(span):
-        row = (summed(near_one, rp_one, j) * valid(j, my_reach)).astype(bf16)
-        for q in range(Q):
-            home[q, j] = row[:, q * KS:(q + 1) * KS]
-    send_parts(home, rx_two, 1, False)
+    arrive_one, close_one = convolve_reduce(wv_one, 0, tx_one, near_one, rp_one)
+    third = span // pieces(span)
+    for ch in range(pieces(span)):
+        arrive_one(ch)
+        for j in range(ch * third, (ch + 1) * third):
+            row = (summed(near_one, rp_one, j) * valid(j, my_reach)).astype(bf16)
+            for q in range(Q):
+                home[q, j] = row[:, q * KS:(q + 1) * KS]
+        send_piece(home, rx_two, 1, ch, False)
     receive_parts(home, rx_two, 1)
     build(window_two, 1, halo_two, st_own_two, st_sib_two)
     loads[1].wait()
-    convolve_reduce(wv_two, 1, tx_two, near_two, rp_two)
+    arrive_two, close_two = convolve_reduce(wv_two, 1, tx_two, near_two, rp_two)
 
     @pl.when(z > 0)
     def _():
@@ -404,9 +442,12 @@
     def _():
         edge.wait_recv()
 
-    send_parts(lat, rx_one, 0, True)
-    send_parts(home, rx_two, 1, True)
-    for j in reversed(range(span)):
+    finish_parts(lat, rx_one, 0)
+    finish_parts(home, rx_two, 1)
+    close_one()
+    for ch in range(pieces(span)):
+        arrive_two(ch)
+    for j in range(span):
         row = summed(near_two, rp_two, j)
         for q in range(Q):
             base = lat[q, j] if j < B else inc[q, j - B]
@@ -438,6 +479,8 @@
         else:
             for q in range(Q):
                 out[q, j] = ys[q, j // 2]
+
+    close_two()
 
     @pl.when(z < T - 1)
     def _():
@@ -471,8 +514,8 @@
         vm((pairs, span * FR, CL), bf16), vm((pairs, span * FR, CL), bf16),
         vm((pairs, span * FR, CL), bf16), vm((pairs, span * FR, CL), bf16),
         vm((Q, span, FR, KS), bf16), vm((Q, span, FR, KS), bf16), vm((Q, INTERSECTION, FR, KS), bf16),
-        dma((2,)), dma((2, Q)), dma((2, T)), dma((2, C, T)), dma((2,)), dma((C,)), dma((C,)), dma((2, 2)), dma((2, 2)),
-        dma((2, T)), dma((2, T)), dma((2,)),
+        dma((2,)), dma((2, Q, 3)), dma((2, T, 3)), dma((2, C, T, 3)), dma((2,)), dma((C,)), dma((C,)), dma((2, 2)), dma((2, 2)),
+        dma((2, T, 3)), dma((2, T, 3)), dma((2,)),
     ]
     whole = pl.BlockSpec(memory_space=pltpu.VMEM)
     result = pl.pallas_call(

time: 68 us -> 65.6 us (0.965)
  Pallas kernels: 62.9 us -> 60.5 us
    pallas_call x1, Pallas kernels: 62.9 us -> 60.5 us  [stationary(): pl.pallas_call(functools.partial(block_kernel, (T, C, Q, B, F, R, KS, CL,...]
where the time goes in v4:
time: 65.6 us; the launch traced here: 65.4 us
  Pallas kernels  60.5 us (92%)
  local copies, waits for them, and re-layouts  3.57 us (5%)
  other arithmetic  1.3 us (2%)
    pallas_call x1, Pallas kernels, stationary(): pl.pallas_call(functools.partial(block_kernel, (T, C, Q, B, F, R, KS, CL,...  60.5 us

profile of v4, /device:TPU:0, one launch (start us, length us, event | category | flops | bytes accessed | tf_op | source)
XLA Modules:
  0.0 65.4 jit_solution(3284760217619952660)
XLA Ops:
  0.0 1.3 %select_maximum_fusion.gains = f32[2,8,128]{2,1,0:T(8,128)} fusion(f32[2,1,128]{2,1,0:T(1,128)} %bitcast.23, f32[2,1,128]{2,1,0:T(1,128)} %bitcast.24), kind=kLoop, calls=%fused_computation.2 | loop fusion | flops 8192 | bytes 10240 | tf_op jit(solution)/shard_map/stack | solution.py:499
  1.3 0.9 %copy.7 = bf16[4,8,5,256]{3,1,0,2:T(8,128)(2,1)S(1)} copy(bf16[4,8,5,256]{3,1,2,0:T(8,128)(2,1)} %param.6) | data formatting | bytes 163840 | tf_op args[0]
  2.2 0.7 copy.12
  2.9 60.5 %shard_map.64 = bf16[2,10,32,128]{3,2,1,0:T(8,128)(2,1)} custom-call(s32[4]{0:T(128)} %reach_ref.1, bf16[2,5,32,128]{3,2,1,0:T(8,128)(2,1)} %bitcast.22, f32[2,8,128]{2,1,0:T(8,128)} %select_maximum_fusion.gains, bf16[3456,256]{1,0:T(8,128)(2,1)} %bitcast.20, bf16[3456,256]{1,0:T(8,128)(2,1)} %bitcast.21), custom_call_target="tpu_custom_call" | custom-call | tf_op jit(solution)/shard_map/pallas_call | solution.py:521
  63.3 0.9 %copy_bitcast_fusion = bf16[4,8,10,256]{3,1,2,0:T(8,128)(2,1)S(1)} fusion(bf16[2,10,32,128]{3,2,1,0:T(8,128)(2,1)} %shard_map.64), kind=kLoop, calls=%fused_computation | loop fusion | bytes 327680 | tf_op jit(solution)/shard_map/reshape | solution.py:532
  64.3 0.2 broadcast_in_dim.3
  64.5 0.9 %reshape.23 = bf16[4,16,10,256]{3,1,2,0:T(8,128)(2,1)} reshape(bf16[4,8,2,10,256]{4,2,1,3,0:T(2,128)(2,1)S(1)} %broadcast_in_dim.3) | data formatting | bytes 655360 | tf_op jit(solution)/shard_map/reshape | solution.py:533
  (1 shorter events, 0.0 us)

commit v5 on v4

--- a/solution.py
+++ b/solution.py
@@ -117,7 +117,7 @@
 bf16 = jnp.bfloat16
 
 
-def block_kernel(dims, reach_ref, lat, gains, w_one, w_two, out, rx_one, rx_two, inc, gx, halo_one, halo_two,
+def block_kernel(dims, reach_ref, lat_in, g_one, g_two, w_one, w_two, out, rx_one, rx_two, inc, lat, gains, gx, halo_one, halo_two,
                  st_own_one, st_own_two, st_sib_one, st_sib_two, xs, hs, wv_one, wv_two, tx_one, tx_two, near_one,
                  near_two, rp_one, rp_two, home, ys, tail, w_sem, dist_send, dist_recv, fwd_send, inc_sem, gain_send, gain_recv, halo_sem,
                  st_sem, red_send, red_recv, tail_sem):
@@ -152,6 +152,11 @@
     pl.semaphore_signal(barrier, inc=1, device_id=(g, z, c, sib), device_id_type=MESH)
     pl.semaphore_wait(barrier, T * C)
 
+    for j in range(B):
+        column = lat_in[:, j].astype(f32).reshape(FR, CL).astype(bf16)
+        for q in range(Q):
+            lat[q, j] = column[:, q * KS:(q + 1) * KS]
+
     def pieces(columns):
         return 3 if columns % 3 == 0 else 1
 
@@ -225,6 +230,9 @@
     def _():
         inc[...] = jnp.zeros_like(inc)
 
+    for q in range(Q):
+        gains[q] = jnp.broadcast_to(g_one[q:q + 1], (8, KS))
+        gains[q, 1:2] = g_two[q:q + 1]
     gx[c] = gains[...]
     for cc in range(C):
         @pl.when(c != cc)
@@ -327,7 +335,7 @@
                 hs[2, p, j + 1] = up.reshape(F + 2, 2 * R, KS).astype(bf16)
                 return carry
 
-            lax.fori_loop(0, span, column, 0)
+            lax.fori_loop(0, span, column, 0, unroll=3 if span % 3 == 0 else 1)
 
     rows_m = span * F * 2 * R
 
@@ -495,9 +503,7 @@
     span = B + INTERSECTION
     FR = F * R
     pairs = T // 2
-    lat = latent.reshape(FR, B, Q, KS).transpose(2, 1, 0, 3)
-    gains = jnp.stack([gain_one.reshape(Q, KS), gain_two.reshape(Q, KS)], axis=1)
-    gains = jnp.pad(gains, ((0, 0), (0, 6), (0, 0)))
+    lat = latent.transpose(0, 2, 1, 3)
     taps = weight_one.shape[0] * weight_one.shape[1] * weight_one.shape[2]
     w_one = weight_one.reshape(taps * KS, CL)
     w_two = weight_two.reshape(taps * KS, CL)
@@ -505,7 +511,7 @@
     dma = pltpu.SemaphoreType.DMA
     scratch = [
         vm((T, B, FR, KS), bf16), vm((T, span, FR, KS), bf16), vm((Q, INTERSECTION, FR, KS), bf16),
-        vm((C, Q, 8, KS), f32),
+        vm((Q, B, FR, KS), bf16), vm((Q, 8, KS), f32), vm((C, Q, 8, KS), f32),
         vm((pairs, span, 2, 2 * R, KS), bf16), vm((pairs, span, 2, 2 * R, KS), bf16),
         vm((2, T * R, KS), f32), vm((2, T * R, KS), f32), vm((2, T * R, KS), f32), vm((2, T * R, KS), f32),
         vm((pairs, span, F, 2 * R, KS), bf16), vm((3, pairs, span + 2, F + 2, 2 * R, KS), bf16),
@@ -521,14 +527,14 @@
     result = pl.pallas_call(
         functools.partial(block_kernel, (T, C, Q, B, F, R, KS, CL, span)),
         out_shape=jax.ShapeDtypeStruct((Q, 2 * B, FR, KS), bf16),
-        in_specs=[pl.BlockSpec(memory_space=pltpu.SMEM), whole, whole,
+        in_specs=[pl.BlockSpec(memory_space=pltpu.SMEM), whole, whole, whole,
                   pl.BlockSpec(memory_space=pl.ANY), pl.BlockSpec(memory_space=pl.ANY)],
         out_specs=whole,
         scratch_shapes=scratch,
         compiler_params=pltpu.CompilerParams(
             collective_id=0, has_side_effects=True, vmem_limit_bytes=60 * 1024 * 1024
         ),
-    )(extents, lat, gains, w_one, w_two)
+    )(extents, lat, gain_one.reshape(Q, KS), gain_two.reshape(Q, KS), w_one, w_two)
     result = result.reshape(Q, 2 * B, F, R, KS).transpose(2, 3, 1, 0, 4).reshape(F, R, 2 * B, CL)
     return jnp.repeat(result, 2, axis=1)
 

time: 65.6 us -> 62.1 us (0.947)
  local copies, waits for them, and re-layouts: 3.57 us -> 2 us
  other arithmetic: 1.3 us -> 0 us
    another operation x1 -> x0, other arithmetic: 1.3 us -> none  [stationary(): jnp.stack([gain_one.reshape(Q, KS), gain_two.reshape(Q, KS)], axis=1)]
    unnamed x1 -> x0, local copies, waits for them, and re-layouts: 0.89 us -> none
    reshape x2 -> x0, local copies, waits for them, and re-layouts: 0.68 us -> none  [stationary(): lat = latent.reshape(FR, B, Q, KS).transpose(2, 1, 0, 3)]
where the time goes in v5:
time: 62.1 us; the launch traced here: 61.9 us
  Pallas kernels  59.9 us (96%)
  local copies, waits for them, and re-layouts  2 us (3%)
    pallas_call x1, Pallas kernels, stationary(): pl.pallas_call(functools.partial(block_kernel, (T, C, Q, B, F, R, KS, CL,...  59.9 us

profile of v5, /device:TPU:0, one launch (start us, length us, event | category | flops | bytes accessed | tf_op | source)
XLA Modules:
  0.0 61.9 jit_solution(14556948405632045034)
XLA Ops:
  0.0 59.9 %shard_map.64 = bf16[2,10,32,128]{3,2,1,0:T(8,128)(2,1)} custom-call(s32[4]{0:T(128)} %reach_ref.1, bf16[4,5,8,256]{3,2,1,0:T(8,128)(2,1)} %bitcast.16, f32[2,128]{1,0:T(2,128)} %bitcast.17, f32[2,128]{1,0:T(2,128)} %bitcast.18, bf16[3456,256]{1,0:T(8,128)(2,1)} %bitcast.14, bf16[3456,256]{1,0:T(8,128)(2,1)} %bitcast.15), custom_call_target="tpu_custom_call" | custom-call | tf_op jit(solution)/shard_map/pallas_call | solution.py:527
  59.9 0.9 %copy_bitcast_fusion = bf16[4,8,10,256]{3,1,2,0:T(8,128)(2,1)S(1)} fusion(bf16[2,10,32,128]{3,2,1,0:T(8,128)(2,1)} %shard_map.64), kind=kLoop, calls=%fused_computation | loop fusion | bytes 327680 | tf_op jit(solution)/shard_map/reshape | solution.py:538
  60.8 0.2 broadcast_in_dim.3
  61.1 0.9 %reshape.27 = bf16[4,16,10,256]{3,1,2,0:T(8,128)(2,1)} reshape(bf16[4,8,2,10,256]{4,2,1,3,0:T(2,128)(2,1)S(1)} %broadcast_in_dim.3) | data formatting | bytes 655360 | tf_op jit(solution)/shard_map/reshape | solution.py:539

commit v6 on v5

--- a/solution.py
+++ b/solution.py
@@ -335,7 +335,7 @@
                 hs[2, p, j + 1] = up.reshape(F + 2, 2 * R, KS).astype(bf16)
                 return carry
 
-            lax.fori_loop(0, span, column, 0, unroll=3 if span % 3 == 0 else 1)
+            lax.fori_loop(0, span, column, 0, unroll=True)
 
     rows_m = span * F * 2 * R
 
@@ -483,10 +483,11 @@
             ramp = jnp.where(spot < limit, spot / jnp.maximum(limit, 2.0), 1.0)
             for q in range(Q):
                 mixed = ys[q, j // 2].astype(f32) * ramp + tail[q, j // 2].astype(f32) * (1.0 - ramp)
-                out[q, j] = mixed.astype(bf16)
+                out[:, j, :, q * KS:(q + 1) * KS] = mixed.reshape(F, R, KS).astype(bf16)
         else:
             for q in range(Q):
-                out[q, j] = ys[q, j // 2]
+                plain = ys[q, j // 2].astype(f32).reshape(F, R, KS)
+                out[:, j, :, q * KS:(q + 1) * KS] = plain.astype(bf16)
 
     close_two()
 
@@ -526,7 +527,7 @@
     whole = pl.BlockSpec(memory_space=pltpu.VMEM)
     result = pl.pallas_call(
         functools.partial(block_kernel, (T, C, Q, B, F, R, KS, CL, span)),
-        out_shape=jax.ShapeDtypeStruct((Q, 2 * B, FR, KS), bf16),
+        out_shape=jax.ShapeDtypeStruct((F, 2 * B, R, CL), bf16),
         in_specs=[pl.BlockSpec(memory_space=pltpu.SMEM), whole, whole, whole,
                   pl.BlockSpec(memory_space=pl.ANY), pl.BlockSpec(memory_space=pl.ANY)],
         out_specs=whole,
@@ -535,8 +536,7 @@
             collective_id=0, has_side_effects=True, vmem_limit_bytes=60 * 1024 * 1024
         ),
     )(extents, lat, gain_one.reshape(Q, KS), gain_two.reshape(Q, KS), w_one, w_two)
-    result = result.reshape(Q, 2 * B, F, R, KS).transpose(2, 3, 1, 0, 4).reshape(F, R, 2 * B, CL)
-    return jnp.repeat(result, 2, axis=1)
+    return jnp.repeat(result.transpose(0, 2, 1, 3), 2, axis=1)
 
 
 def choose(latent, extents, gain_one, weight_one, gain_two, weight_two):

time: 62.1 us -> 61.9 us (level)
    reshape x2 -> x1, local copies, waits for them, and re-layouts: 1.79 us -> 0.85 us  [stationary(): return jnp.repeat(result.transpose(0, 2, 1, 3), 2, axis=1)]
    broadcast_in_dim x1, local copies, waits for them, and re-layouts: 0.21 us -> 1.11 us  [stationary(): return jnp.repeat(result.transpose(0, 2, 1, 3), 2, axis=1)]
where the time goes in v6:
time: 61.9 us; the launch traced here: 61.8 us
  Pallas kernels  59.8 us (97%)
  local copies, waits for them, and re-layouts  1.96 us (3%)
    pallas_call x1, Pallas kernels, stationary(): pl.pallas_call(functools.partial(block_kernel, (T, C, Q, B, F, R, KS, CL,...  59.8 us

profile of v6, /device:TPU:0, one launch (start us, length us, event | category | flops | bytes accessed | tf_op | source)
XLA Modules:
  0.0 61.8 jit_solution(5886999034689490706)
XLA Ops:
  0.0 59.8 %shard_map.64 = bf16[4,10,8,256]{3,2,1,0:T(8,128)(2,1)} custom-call(s32[4]{0:T(128)} %reach_ref.1, bf16[4,5,8,256]{3,2,1,0:T(8,128)(2,1)} %bitcast.11, f32[2,128]{1,0:T(2,128)} %bitcast.12, f32[2,128]{1,0:T(2,128)} %bitcast.13, bf16[3456,256]{1,0:T(8,128)(2,1)} %bitcast.8, bf16[3456,256]{1,0:T(8,128)(2,1)} %bitcast.9), custom_call_target="tpu_custom_call" | custom-call | tf_op jit(solution)/shard_map/pallas_call | solution.py:528
  59.8 1.1 %broadcast_in_dim.3 = bf16[4,8,2,10,256]{4,2,1,3,0:T(2,128)(2,1)S(1)} broadcast(bf16[4,8,10,256]{3,1,2,0:T(8,128)(2,1)} %bitcast.10), dimensions={0,1,3,4} | broadcast | bytes 491520 | tf_op jit(solution)/shard_map/broadcast_in_dim | solution.py:539
  60.9 0.9 %reshape.19 = bf16[4,16,10,256]{3,1,2,0:T(8,128)(2,1)} reshape(bf16[4,8,2,10,256]{4,2,1,3,0:T(2,128)(2,1)S(1)} %broadcast_in_dim.3) | data formatting | bytes 655360 | tf_op jit(solution)/shard_map/reshape | solution.py:539
